TPU v7x, 128 devices: a whole 4x4x4 slice. The times are simulated.
128 devices in a mesh: scene: 8 (over y, core), frame: 16 (over z, x).
Axes of the slice: x: 4, y: 4, z: 4, core: 2. Of those that a mesh axis runs over, the one named last changes fastest.
Arguments:
- occupancy: bfloat16 [8, 64, 64, 2048], P('scene', 'frame'), may hold values from -6 to 6
- scene_lengths: int32 [8], P('scene'), may hold values from 8 to 64, as said below
- conv1_weight: bfloat16 [128, 1728], replicated, may hold values from -0.15625 to 0.15625
- conv2_weight: bfloat16 [256, 3456], replicated, may hold values from -0.109375 to 0.109375
- temporal_weight: bfloat16 [3, 256, 256], replicated, may hold values from -0.21875 to 0.21875
- query_weight: bfloat16 [256, 256], replicated
- key_weight: bfloat16 [256, 256], replicated
- value_weight: bfloat16 [256, 256], replicated, may hold values from -0.375 to 0.375
- out_weight: bfloat16 [256, 256], replicated, may hold values from -0.375 to 0.375
Outputs:
- encoded: bfloat16 [8, 64, 256, 512], P('scene', 'frame')
- kl_loss: float32 [], replicated
Inputs may be any that keep to these rules, and one draw needn't show every extreme that they name: `scene_lengths`: non-decreasing along the scenes; the first scene has exactly 8 frames with data and the last exactly 64.
All inputs are finite; a program needn't handle non-finite values.
Results may differ from a plain program's by a relative error of at most 0.011.
Values may be sent and summed in bfloat16 or wider, within the bound.
A program may use at most 192 MiB of HBM per device.

v0:
```python
import jax
import jax.numpy as jnp
from jax import lax
from jax.sharding import PartitionSpec as P

CIN = 64
C1 = 128
C2 = 256
HEADS = 4
HD = 64
HI = 16
ZD = 8
CELLS = 512
NORM_EPS = 1e-06


def spatial_conv(voxels, weight, channels_in, stride):
    channels_out = weight.shape[0]
    kernel = weight.reshape(channels_out, channels_in, 3, 3, 3)
    return lax.conv_general_dilated(
        voxels,
        kernel,
        (stride, stride, 1),
        ((1, 1), (1, 1), (1, 1)),
        dimension_numbers=("NCDHW", "OIDHW", "NCDHW"),
        preferred_element_type=jnp.float32,
    )


def mix(maps, weight):
    return jnp.einsum("tnc,oc->tno", maps, weight, preferred_element_type=jnp.float32)


def shards(
    occupancy,
    scene_lengths,
    conv1_weight,
    conv2_weight,
    temporal_weight,
    query_weight,
    key_weight,
    value_weight,
    out_weight,
):
    f_dev = occupancy.shape[1]
    length = scene_lengths[0]
    first_frame = lax.axis_index("frame") * f_dev
    frame_ids = first_frame + jnp.arange(f_dev, dtype=jnp.int32)
    valid_rows = (frame_ids < length).astype(jnp.float32)
    voxels = occupancy[0].reshape(f_dev, CIN, HI, HI, ZD)
    first_maps = jax.nn.silu(spatial_conv(voxels, conv1_weight, CIN, 2)).astype(jnp.bfloat16)
    second_full = jax.nn.silu(spatial_conv(first_maps, conv2_weight, C1, 1))
    second_maps = (second_full.reshape(f_dev, C2, CELLS) * valid_rows[:, None, None]).astype(
        jnp.bfloat16
    )
    second = lax.all_to_all(second_maps.transpose(0, 2, 1), "frame", 1, 0, tiled=True)
    frames, cells = second.shape[:2]
    padded = jnp.pad(second, ((1, 1), (0, 0), (0, 0)))
    temporal_sum = mix(padded[0:frames], temporal_weight[0])
    for tap in range(1, 3):
        temporal_sum = temporal_sum + mix(padded[tap : tap + frames], temporal_weight[tap])
    residual = (second.astype(jnp.float32) + jax.nn.silu(temporal_sum)).astype(jnp.bfloat16)
    residual = residual.astype(jnp.float32)
    normed = (
        residual * lax.rsqrt(jnp.mean(residual * residual, axis=2, keepdims=True) + NORM_EPS)
    ).astype(jnp.bfloat16)
    split = (frames, cells, HEADS, HD)
    queries = mix(normed, query_weight).astype(jnp.bfloat16).reshape(split)
    keys = mix(normed, key_weight).astype(jnp.bfloat16).reshape(split)
    values = mix(normed, value_weight).astype(jnp.bfloat16).reshape(split)
    scores = jnp.einsum(
        "qnhd,knhd->nhqk", queries, keys, preferred_element_type=jnp.float32
    ) * HD ** (-0.5)
    key_mask = (jnp.arange(frames) < length)[None, None, None, :]
    scores = jnp.where(key_mask, scores, -1e30)
    row_max = jnp.max(scores, axis=3, keepdims=True)
    weights = jnp.where(key_mask, jnp.exp(scores - row_max), 0.0)
    total = jnp.sum(weights, axis=3, keepdims=True)
    weighted = jnp.einsum(
        "nhqk,knhd->nhqd", weights.astype(jnp.bfloat16), values, preferred_element_type=jnp.float32
    )
    attended = (weighted / total).astype(jnp.bfloat16)
    attended = attended.transpose(2, 0, 1, 3).reshape(frames, cells, C2)
    row_valid = (jnp.arange(frames) < length).astype(jnp.float32)[:, None, None]
    encoded = ((residual + mix(attended, out_weight)) * row_valid).astype(jnp.bfloat16)
    squares = jnp.sum(jnp.square(encoded.astype(jnp.float32)))
    grand_total = lax.psum(squares, ("scene", "frame"))
    slot_count = float(lax.axis_size("scene") * frames * CELLS * C2)
    kl_loss = 0.5 * grand_total / slot_count
    encoded = lax.all_to_all(encoded, "frame", 0, 1, tiled=True).transpose(0, 2, 1)
    return (encoded[None], kl_loss)


def solution(mesh):
    placed = (P("scene", "frame", None, None), P("scene"), P(), P(), P(), P(), P(), P(), P())
    return jax.shard_map(
        shards,
        mesh=mesh,
        in_specs=placed,
        out_specs=(P("scene", "frame", None, None), P()),
        check_vma=False,
    )
```

profile of v0, /device:TPU:1, one launch (start us, length us, event | category | flops | bytes accessed | tf_op | source)
XLA Modules:
  0.0 162.8 jit_solution(13435538620634952501)
XLA Ops:
  0.6 0.0 copy-start
  1.3 2.6 %copy.23 = bf16[256,3456]{0,1:T(8,128)(2,1)S(1)} copy(bf16[256,3456]{1,0:T(8,128)(2,1)} %param.12) | data formatting | bytes 3538944 | tf_op args[3]
  4.0 0.0 copy-start.3
  4.0 2.9 %reshape.51 = bf16[256,128,3,3,3]{0,4,3,2,1:T(4,128)(2,1)} reshape(bf16[256,3456]{0,1:T(8,128)(2,1)S(1)} %copy.23) | data formatting | bytes 3538944 | tf_op jit(solution)/shard_map/reshape | solution.py:19
  6.8 0.0 copy-done.3
  6.8 1.1 copy.20
  7.9 1.5 reshape.50
  9.4 0.0 copy-start.1
  9.4 5.0 %fusion.22 = bf16[4,128,8,8,8]{1,0,4,3,2:T(4,128)(2,1)S(1)} fusion(bf16[4,64,16,16,8]{1,4,3,2,0:T(8,128)(2,1)S(1)} %bitcast.70, bf16[128,64,3,3,3]{0,4,3,2,1:T(4,128)(2,1)S(1)} %reshape.50), kind=kOutput, calls=%fused_computation.34 | convolution fusion | flops 764018688 | bytes 2015232 | tf_op jit(solution)/shard_map/conv_general_dilated | solution.py:20
  14.4 0.0 copy-done.1
  14.4 6.6 %divide_multiply_fusion = f32[4,256,8,8,8]{1,0,4,3,2:T(4,128)S(1)} fusion(bf16[4,128,8,8,8]{1,0,4,3,2:T(4,128)(2,1)S(1)} %fusion.22, bf16[256,128,3,3,3]{0,4,3,2,1:T(4,128)(2,1)S(1)} %copy-done.1), kind=kOutput, calls=%fused_computation.9 | convolution fusion | flops 2793406464 | bytes 4390912 | tf_op jit(solution)/shard_map/conv_general_dilated | solution.py:20
  21.0 1.5 fusion.7
  22.6 0.0 copy-start.4
  22.6 8.6 %all-to-all-start = ((bf16[4,512,256]{2,0,1:T(4,128)(2,1)}), bf16[4,512,256]{2,0,1:T(4,128)(2,1)S(1)}, u32[]{:S(2)}, u32[]{:S(2)}) async-start(bf16[4,512,256]{2,0,1:T(4,128)(2,1)} %bitcast.3), calls=%async_computation | async-start | bytes 2097152 | tf_op jit(solution)/shard_map/all_to_all | solution.py:56
  31.2 16.0 %all-to-all-done = bf16[4,512,256]{2,0,1:T(4,128)(2,1)S(1)} async-done(((bf16[4,512,256]{2,0,1:T(4,128)(2,1)}), bf16[4,512,256]{2,0,1:T(4,128)(2,1)S(1)}, u32[]{:S(2)}, u32[]{:S(2)}) %all-to-all-start) | async-done | bytes 1048608 | tf_op jit(solution)/shard_map/all_to_all | solution.py:56
  47.1 0.2 copy.25
  47.3 0.0 copy-done.4
  47.3 0.5 fusion.34
  47.8 0.5 fusion.36
  48.3 0.0 copy-start.5
  48.3 1.1 fusion.3
  49.5 0.0 copy-done.5
  49.5 1.5 convolution_convert_fusion.2
  50.9 0.0 copy-start.6
  50.9 3.4 %reshape.53 = bf16[64,32,4,64]{3,2,1,0:T(4,128)(2,1)S(1)} reshape(bf16[64,32,256]{2,1,0:T(8,128)(2,1)} %convolution_convert_fusion.2) | data formatting | bytes 2097152 | tf_op jit(solution)/shard_map/reshape | solution.py:68
  54.3 0.0 copy-done.6
  54.3 1.5 convolution_convert_fusion.1
  55.8 0.0 copy-start.7
  55.8 4.5 %reshape.54 = bf16[64,32,4,64]{3,2,1,0:T(4,128)(2,1)} reshape(bf16[64,32,256]{2,1,0:T(8,128)(2,1)} %convolution_convert_fusion.1) | data formatting | bytes 2097152 | tf_op jit(solution)/shard_map/reshape | solution.py:69
  60.2 0.0 copy-done.7
  60.2 1.5 convolution_convert_fusion
  61.7 4.4 %reshape.55 = bf16[64,32,4,64]{3,2,1,0:T(4,128)(2,1)} reshape(bf16[64,32,256]{2,1,0:T(8,128)(2,1)} %convolution_convert_fusion) | data formatting | bytes 2097152 | tf_op jit(solution)/shard_map/reshape | solution.py:70
  66.1 4.1 %fusion.9 = f32[32,4,64,64]{2,3,1,0:T(8,128)S(1)} fusion(bf16[64,32,4,64]{3,2,1,0:T(4,128)(2,1)} %reshape.54, bf16[64,32,4,64]{3,2,1,0:T(4,128)(2,1)S(1)} %reshape.53), kind=kOutput, calls=%fused_computation.17 | convolution fusion | flops 67108864 | bytes 4194304 | tf_op jit(solution)/shard_map/qnhd,knhd->nhqk/dot_general | solution.py:71
  70.3 0.0 copy-start.2
  70.3 1.9 %fusion.44 = (f32[32,4,64]{2,1,0:T(4,128)S(1)}, bf16[32,4,64,64]{2,3,1,0:T(8,128)(2,1)S(1)}) fusion(f32[32,4,64,64]{2,3,1,0:T(8,128)S(1)} %fusion.9, pred[64]{0:T(512)(128)(4,1)S(1)} %get-tuple-element.10), kind=kOutput, calls=%fused_computation.54 | output fusion | flops 4194367 | bytes 3178560 | tf_op jit(solution)/shard_map/sub | solution.py:77
  72.2 0.0 copy-done.2
  72.2 3.3 %fusion.1 = bf16[64,32,4,64]{3,0,2,1:T(8,128)(2,1)S(1)} fusion(bf16[64,32,4,64]{3,2,1,0:T(4,128)(2,1)S(1)} %copy-done.2, f32[64,32,4]{0,2,1:T(4,128)S(1)} %bitcast.71, bf16[32,4,64,64]{2,3,1,0:T(8,128)(2,1)S(1)} %get-tuple-element.7), kind=kOutput, calls=%fused_computation.2 | convolution fusion | flops 68157440 | bytes 3178496 | tf_op jit(solution)/shard_map/nhqk,knhd->nhqd/dot_general | solution.py:79
  75.4 1.6 copy.30
  77.1 2.2 %reshape.56 = bf16[64,32,256]{2,1,0:T(8,128)(2,1)} reshape(bf16[64,32,4,64]{3,2,1,0:T(4,128)(2,1)S(1)} %copy.30) | data formatting | bytes 2097152 | tf_op jit(solution)/shard_map/reshape | solution.py:83
  79.2 0.0 copy-done
  79.2 3.5 %multiply_reduce_fusion = (f32[]{:T(128)}, bf16[64,32,256]{2,1,0:T(8,128)(2,1)}) fusion(f32[64]{0:T(128)S(1)} %get-tuple-element.11, bf16[64,32,256]{2,1,0:T(8,128)(2,1)} %reshape.56, bf16[256,256]{1,0:T(8,128)(2,1)S(1)} %copy-done, bf16[64,32,256]{2,1,0:T(8,128)(2,1)S(1)} %get-tuple-element.5), kind=kOutput, calls=%fused_computation.20 | convolution fusion | flops 272105472 | bytes 3277060 | tf_op jit(solution)/shard_map/tnc,oc->tno/dot_general | solution.py:31
  82.7 4.2 %all-to-all-start.1 = ((bf16[64,32,256]{2,1,0:T(8,128)(2,1)}), bf16[64,32,256]{2,1,0:T(8,128)(2,1)S(1)}, u32[]{:S(2)}, u32[]{:S(2)}) async-start(bf16[64,32,256]{2,1,0:T(8,128)(2,1)} %get-tuple-element.9), calls=%async_computation.1 | async-start | bytes 2097152 | tf_op jit(solution)/shard_map/all_to_all | solution.py:90
  86.9 72.7 %psum.7 = f32[]{:T(128)} all-reduce(f32[]{:T(128)} %get-tuple-element.8), channel_id=1, replica_groups=mesh['scene'=8,'frame'=16] {'scene','frame'}, use_global_device_ids=true, to_apply=%region_4.5 | all-reduce | flops 1 | bytes 8 | tf_op jit(solution)/shard_map/psum | solution.py:87
  160.2 0.0 all-to-all-done.1
  160.2 0.1 copy.31
  160.3 1.3 copy.32
  (3 shorter events, 0.0 us)
Async XLA Ops:
  0.6 78.6 %copy-start = (bf16[256,256]{1,0:T(8,128)(2,1)S(1)}, bf16[256,256]{1,0:T(8,128)(2,1)}, u32[]{:S(2)}) copy-start(bf16[256,256]{1,0:T(8,128)(2,1)} %param.17) | copy-start | bytes 393220
  4.0 2.9 %copy-start.3 = (bf16[1,4,64,2048]{3,2,1,0:T(8,128)(2,1)S(1)}, bf16[1,4,64,2048]{3,2,1,0:T(8,128)(2,1)}, u32[]{:S(2)}) copy-start(bf16[1,4,64,2048]{3,2,1,0:T(8,128)(2,1)} %param.9) | copy-start | bytes 3145732
  9.4 5.0 %copy-start.1 = (bf16[256,128,3,3,3]{0,4,3,2,1:T(4,128)(2,1)S(1)}, bf16[256,128,3,3,3]{0,4,3,2,1:T(4,128)(2,1)}, u32[]{:S(2)}) copy-start(bf16[256,128,3,3,3]{0,4,3,2,1:T(4,128)(2,1)} %reshape.51) | copy-start | bytes 5308420
  22.6 24.8 %copy-start.4 = (bf16[3,256,256]{2,1,0:T(8,128)(2,1)S(1)}, bf16[3,256,256]{2,1,0:T(8,128)(2,1)}, u32[]{:S(2)}) copy-start(bf16[3,256,256]{2,1,0:T(8,128)(2,1)} %param.13) | copy-start | bytes 1179652
  22.6 24.6 %all-to-all-start = ((bf16[4,512,256]{2,0,1:T(4,128)(2,1)}), bf16[4,512,256]{2,0,1:T(4,128)(2,1)S(1)}, u32[]{:S(2)}, u32[]{:S(2)}) async-start(bf16[4,512,256]{2,0,1:T(4,128)(2,1)} %bitcast.3), calls=%async_computation | async-start | bytes 2097152 | tf_op jit(solution)/shard_map/all_to_all | solution.py:56
  48.3 1.2 copy-start.5
  50.9 3.4 %copy-start.6 = (bf16[256,256]{1,0:T(8,128)(2,1)S(1)}, bf16[256,256]{1,0:T(8,128)(2,1)}, u32[]{:S(2)}) copy-start(bf16[256,256]{1,0:T(8,128)(2,1)} %param.15) | copy-start | bytes 393220
  55.8 4.5 %copy-start.7 = (bf16[256,256]{1,0:T(8,128)(2,1)S(1)}, bf16[256,256]{1,0:T(8,128)(2,1)}, u32[]{:S(2)}) copy-start(bf16[256,256]{1,0:T(8,128)(2,1)} %param.16) | copy-start | bytes 393220
  70.3 1.9 %copy-start.2 = (bf16[64,32,4,64]{3,2,1,0:T(4,128)(2,1)S(1)}, bf16[64,32,4,64]{3,2,1,0:T(4,128)(2,1)}, u32[]{:S(2)}) copy-start(bf16[64,32,4,64]{3,2,1,0:T(4,128)(2,1)} %reshape.55) | copy-start | bytes 3145732
  82.7 77.5 %all-to-all-start.1 = ((bf16[64,32,256]{2,1,0:T(8,128)(2,1)}), bf16[64,32,256]{2,1,0:T(8,128)(2,1)S(1)}, u32[]{:S(2)}, u32[]{:S(2)}) async-start(bf16[64,32,256]{2,1,0:T(8,128)(2,1)} %get-tuple-element.9), calls=%async_computation.1 | async-start | bytes 2097152 | tf_op jit(solution)/shard_map/all_to_all | solution.py:90
where the time goes:
time: 163 us
  blocking collectives  72.7 us (45%)
  matrix products  28.9 us (18%)
  local copies, waits for them, and re-layouts  25.7 us (16%)
  waiting for transfers between devices  16 us (10%)
  starting transfers between devices  12.8 us (8%)
  other arithmetic  3.44 us (2%)
  between operations  3.32 us (2%)
    psum x1, blocking collectives, shards(): grand_total = lax.psum(squares, ('scene', 'frame'))  72.7 us
    all_to_all x1, waiting for transfers between devices, shards(): lax.all_to_all(second_maps.transpose(0, 2, 1), 'frame', 1, 0, tiled=True)  16 us
    conv_general_dilated x2, matrix products, spatial_conv(): lax.conv_general_dilated(voxels, kernel, (stride, stride, 1), ((1, 1), (1...  11.6 us
    dot_general x7, matrix products, mix(): jnp.einsum('tnc,oc->tno', maps, weight, preferred_element_type=jnp.float32)  9.93 us
    all_to_all x1, starting transfers between devices, shards(): lax.all_to_all(second_maps.transpose(0, 2, 1), 'frame', 1, 0, tiled=True)  8.57 us
    unnamed x19, local copies, waits for them, and re-layouts  5.05 us
    reshape x1, local copies, waits for them, and re-layouts, shards(): keys = mix(normed, key_weight).astype(jnp.bfloat16).reshape(split)  4.45 us
    reshape x1, local copies, waits for them, and re-layouts, shards(): values = mix(normed, value_weight).astype(jnp.bfloat16).reshape(split)  4.44 us
  transfers between devices with their start and end apart: 2, of which 1 were waited for; matrix products, arithmetic and copies ran while one was open for 0% of the time, Pallas kernels for 0%

commit v1 on v0

--- a/solution.py
+++ b/solution.py
@@ -12,6 +12,12 @@
 ZD = 8
 CELLS = 512
 NORM_EPS = 1e-06
+
+
+def trade_parts(x, mesh_axis, split, join):
+    pieces = jnp.split(x, lax.axis_size(mesh_axis), axis=split)
+    got = lax.all_to_all(jnp.stack(pieces), mesh_axis, 0, 0)
+    return jnp.concatenate(got, axis=join)
 
 
 def spatial_conv(voxels, weight, channels_in, stride):
@@ -53,7 +59,7 @@
     second_maps = (second_full.reshape(f_dev, C2, CELLS) * valid_rows[:, None, None]).astype(
         jnp.bfloat16
     )
-    second = lax.all_to_all(second_maps.transpose(0, 2, 1), "frame", 1, 0, tiled=True)
+    second = trade_parts(second_maps.transpose(0, 2, 1), "frame", 1, 0)
     frames, cells = second.shape[:2]
     padded = jnp.pad(second, ((1, 1), (0, 0), (0, 0)))
     temporal_sum = mix(padded[0:frames], temporal_weight[0])

time: 163 us -> 173 us (1.061)
  local copies, waits for them, and re-layouts: 25.7 us -> 36.2 us
    unnamed x19 -> x34, local copies, waits for them, and re-layouts: 5.05 us -> 14.8 us
where the time goes in v1:
time: 173 us; the launch traced here: 172 us
  blocking collectives  72.7 us (42%)
  local copies, waits for them, and re-layouts  36.2 us (21%)
  matrix products  28.9 us (17%)
  waiting for transfers between devices  16 us (9%)
  starting transfers between devices  12.8 us (7%)
  between operations  3.33 us (2%)
  other arithmetic  2.47 us (1%)
    psum x1, blocking collectives, shards(): grand_total = lax.psum(squares, ('scene', 'frame'))  72.7 us
    all_to_all x1, waiting for transfers between devices, trade_parts(): got = lax.all_to_all(jnp.stack(pieces), mesh_axis, 0, 0)  16 us
    unnamed x34, local copies, waits for them, and re-layouts  14.8 us
    conv_general_dilated x2, matrix products, spatial_conv(): lax.conv_general_dilated(voxels, kernel, (stride, stride, 1), ((1, 1), (1...  11.6 us
    dot_general x7, matrix products, mix(): jnp.einsum('tnc,oc->tno', maps, weight, preferred_element_type=jnp.float32)  9.93 us
    all_to_all x1, starting transfers between devices, trade_parts(): got = lax.all_to_all(jnp.stack(pieces), mesh_axis, 0, 0)  8.57 us
    reshape x1, local copies, waits for them, and re-layouts, shards(): keys = mix(normed, key_weight).astype(jnp.bfloat16).reshape(split)  4.45 us
    reshape x1, local copies, waits for them, and re-layouts, shards(): values = mix(normed, value_weight).astype(jnp.bfloat16).reshape(split)  4.44 us
  transfers between devices with their start and end apart: 2, of which 1 were waited for; matrix products, arithmetic and copies ran while one was open for 0% of the time, Pallas kernels for 0%

profile of v1, /device:TPU:1, one launch (start us, length us, event | category | flops | bytes accessed | tf_op | source)
XLA Modules:
  0.0 172.3 jit_solution(8227732353783583039)
XLA Ops:
  0.6 0.0 copy-start
  1.3 2.6 %copy.23 = bf16[256,3456]{0,1:T(8,128)(2,1)S(1)} copy(bf16[256,3456]{1,0:T(8,128)(2,1)} %param.12) | data formatting | bytes 3538944 | tf_op args[3]
  4.0 0.0 copy-start.3
  4.0 2.9 %reshape.54 = bf16[256,128,3,3,3]{0,4,3,2,1:T(4,128)(2,1)} reshape(bf16[256,3456]{0,1:T(8,128)(2,1)S(1)} %copy.23) | data formatting | bytes 3538944 | tf_op jit(solution)/shard_map/reshape | solution.py:25
  6.8 1.1 copy.20
  7.9 1.5 reshape.53
  9.4 5.0 %fusion.22 = bf16[4,128,8,8,8]{1,0,4,3,2:T(4,128)(2,1)S(1)} fusion(bf16[4,64,16,16,8]{1,4,3,2,0:T(8,128)(2,1)S(1)} %bitcast.146, bf16[128,64,3,3,3]{0,4,3,2,1:T(4,128)(2,1)S(1)} %reshape.53), kind=kOutput, calls=%fused_computation.34 | convolution fusion | flops 764018688 | bytes 2015232 | tf_op jit(solution)/shard_map/conv_general_dilated | solution.py:26
  14.4 6.6 %divide_multiply_fusion = f32[4,256,8,8,8]{1,0,4,3,2:T(4,128)S(1)} fusion(bf16[4,128,8,8,8]{1,0,4,3,2:T(4,128)(2,1)S(1)} %fusion.22, bf16[256,128,3,3,3]{0,4,3,2,1:T(4,128)(2,1)S(1)} %copy-done.1), kind=kOutput, calls=%fused_computation.9 | convolution fusion | flops 2793406464 | bytes 4390912 | tf_op jit(solution)/shard_map/conv_general_dilated | solution.py:26
  21.0 0.6 fusion.7
  21.6 0.7 fusion.56
  22.3 0.7 fusion.55
  22.9 0.7 fusion.54
  23.6 0.7 fusion.53
  24.2 0.7 fusion.52
  24.9 0.7 fusion.51
  25.5 0.7 fusion.50
  26.2 0.7 fusion.49
  26.8 0.7 fusion.48
  27.5 0.7 fusion.47
  28.1 0.7 fusion.46
  28.8 0.7 fusion.45
  29.4 0.7 fusion.44
  30.1 0.7 fusion.43
  30.8 0.7 fusion.42
  31.4 0.7 fusion.41
  32.1 8.6 %all-to-all-start = ((bf16[16,4,32,256]{3,1,2,0:T(4,128)(2,1)}), bf16[16,4,32,256]{3,1,2,0:T(4,128)(2,1)S(1)}, u32[]{:S(2)}, u32[]{:S(2)}) async-start(bf16[16,4,32,256]{3,1,2,0:T(4,128)(2,1)} %fusion.41), calls=%async_computation | async-start | bytes 2097152 | tf_op jit(solution)/shard_map/all_to_all | solution.py:19
  40.7 16.0 %all-to-all-done = bf16[16,4,32,256]{3,1,2,0:T(4,128)(2,1)S(1)} async-done(((bf16[16,4,32,256]{3,1,2,0:T(4,128)(2,1)}), bf16[16,4,32,256]{3,1,2,0:T(4,128)(2,1)S(1)}, u32[]{:S(2)}, u32[]{:S(2)}) %all-to-all-start) | async-done | bytes 1048608 | tf_op jit(solution)/shard_map/all_to_all | solution.py:19
  56.6 0.2 copy.25
  56.8 0.5 fusion.34
  57.3 0.5 fusion.36
  57.8 0.0 copy-start.5
  57.8 1.1 fusion.3
  59.0 1.5 convolution_convert_fusion.2
  60.4 3.4 %reshape.57 = bf16[64,32,4,64]{3,2,1,0:T(4,128)(2,1)S(1)} reshape(bf16[64,32,256]{2,1,0:T(8,128)(2,1)} %convolution_convert_fusion.2) | data formatting | bytes 2097152 | tf_op jit(solution)/shard_map/reshape | solution.py:74
  63.8 1.5 convolution_convert_fusion.1
  65.3 4.5 %reshape.58 = bf16[64,32,4,64]{3,2,1,0:T(4,128)(2,1)} reshape(bf16[64,32,256]{2,1,0:T(8,128)(2,1)} %convolution_convert_fusion.1) | data formatting | bytes 2097152 | tf_op jit(solution)/shard_map/reshape | solution.py:75
  69.7 1.5 convolution_convert_fusion
  71.2 4.4 %reshape.59 = bf16[64,32,4,64]{3,2,1,0:T(4,128)(2,1)} reshape(bf16[64,32,256]{2,1,0:T(8,128)(2,1)} %convolution_convert_fusion) | data formatting | bytes 2097152 | tf_op jit(solution)/shard_map/reshape | solution.py:76
  75.6 4.1 %fusion.9 = f32[32,4,64,64]{2,3,1,0:T(8,128)S(1)} fusion(bf16[64,32,4,64]{3,2,1,0:T(4,128)(2,1)} %reshape.58, bf16[64,32,4,64]{3,2,1,0:T(4,128)(2,1)S(1)} %reshape.57), kind=kOutput, calls=%fused_computation.17 | convolution fusion | flops 67108864 | bytes 4194304 | tf_op jit(solution)/shard_map/qnhd,knhd->nhqk/dot_general | solution.py:77
  79.8 1.9 %fusion.60 = (f32[32,4,64]{2,1,0:T(4,128)S(1)}, bf16[32,4,64,64]{2,3,1,0:T(8,128)(2,1)S(1)}) fusion(f32[32,4,64,64]{2,3,1,0:T(8,128)S(1)} %fusion.9, pred[64]{0:T(512)(128)(4,1)S(1)} %get-tuple-element.10), kind=kOutput, calls=%fused_computation.86 | output fusion | flops 4194367 | bytes 3178560 | tf_op jit(solution)/shard_map/sub | solution.py:83
  81.7 3.3 %fusion.1 = bf16[64,32,4,64]{3,0,2,1:T(8,128)(2,1)S(1)} fusion(bf16[64,32,4,64]{3,2,1,0:T(4,128)(2,1)S(1)} %copy-done.2, f32[64,32,4]{0,2,1:T(4,128)S(1)} %bitcast.147, bf16[32,4,64,64]{2,3,1,0:T(8,128)(2,1)S(1)} %get-tuple-element.7), kind=kOutput, calls=%fused_computation.2 | convolution fusion | flops 68157440 | bytes 3178496 | tf_op jit(solution)/shard_map/nhqk,knhd->nhqd/dot_general | solution.py:85
  84.9 1.6 copy.30
  86.6 2.2 %reshape.60 = bf16[64,32,256]{2,1,0:T(8,128)(2,1)} reshape(bf16[64,32,4,64]{3,2,1,0:T(4,128)(2,1)S(1)} %copy.30) | data formatting | bytes 2097152 | tf_op jit(solution)/shard_map/reshape | solution.py:89
  88.7 3.5 %multiply_reduce_fusion = (f32[]{:T(128)}, bf16[64,32,256]{2,1,0:T(8,128)(2,1)}) fusion(f32[64]{0:T(128)S(1)} %get-tuple-element.11, bf16[64,32,256]{2,1,0:T(8,128)(2,1)} %reshape.60, bf16[256,256]{1,0:T(8,128)(2,1)S(1)} %copy-done, bf16[64,32,256]{2,1,0:T(8,128)(2,1)S(1)} %get-tuple-element.5), kind=kOutput, calls=%fused_computation.20 | convolution fusion | flops 272105472 | bytes 3277060 | tf_op jit(solution)/shard_map/tnc,oc->tno/dot_general | solution.py:37
  92.2 4.2 %all-to-all-start.1 = ((bf16[64,32,256]{2,1,0:T(8,128)(2,1)}), bf16[64,32,256]{2,1,0:T(8,128)(2,1)S(1)}, u32[]{:S(2)}, u32[]{:S(2)}) async-start(bf16[64,32,256]{2,1,0:T(8,128)(2,1)} %get-tuple-element.9), calls=%async_computation.1 | async-start | bytes 2097152 | tf_op jit(solution)/shard_map/all_to_all | solution.py:96
  96.4 72.7 %psum.7 = f32[]{:T(128)} all-reduce(f32[]{:T(128)} %get-tuple-element.8), channel_id=1, replica_groups=mesh['scene'=8,'frame'=16] {'scene','frame'}, use_global_device_ids=true, to_apply=%region_4.5 | all-reduce | flops 1 | bytes 8 | tf_op jit(solution)/shard_map/psum | solution.py:93
  169.7 0.1 copy.31
  169.8 1.3 copy.32
  (17 shorter events, 0.1 us)
Async XLA Ops:
  0.6 88.1 %copy-start = (bf16[256,256]{1,0:T(8,128)(2,1)S(1)}, bf16[256,256]{1,0:T(8,128)(2,1)}, u32[]{:S(2)}) copy-start(bf16[256,256]{1,0:T(8,128)(2,1)} %param.17) | copy-start | bytes 393220
  4.0 2.9 %copy-start.3 = (bf16[1,4,64,2048]{3,2,1,0:T(8,128)(2,1)S(1)}, bf16[1,4,64,2048]{3,2,1,0:T(8,128)(2,1)}, u32[]{:S(2)}) copy-start(bf16[1,4,64,2048]{3,2,1,0:T(8,128)(2,1)} %param.9) | copy-start | bytes 3145732
  9.4 5.0 %copy-start.1 = (bf16[256,128,3,3,3]{0,4,3,2,1:T(4,128)(2,1)S(1)}, bf16[256,128,3,3,3]{0,4,3,2,1:T(4,128)(2,1)}, u32[]{:S(2)}) copy-start(bf16[256,128,3,3,3]{0,4,3,2,1:T(4,128)(2,1)} %reshape.54) | copy-start | bytes 5308420
  32.1 24.8 %copy-start.4 = (bf16[3,256,256]{2,1,0:T(8,128)(2,1)S(1)}, bf16[3,256,256]{2,1,0:T(8,128)(2,1)}, u32[]{:S(2)}) copy-start(bf16[3,256,256]{2,1,0:T(8,128)(2,1)} %param.13) | copy-start | bytes 1179652
  32.1 24.6 %all-to-all-start = ((bf16[16,4,32,256]{3,1,2,0:T(4,128)(2,1)}), bf16[16,4,32,256]{3,1,2,0:T(4,128)(2,1)S(1)}, u32[]{:S(2)}, u32[]{:S(2)}) async-start(bf16[16,4,32,256]{3,1,2,0:T(4,128)(2,1)} %fusion.41), calls=%async_computation | async-start | bytes 2097152 | tf_op jit(solution)/shard_map/all_to_all | solution.py:19
  57.8 1.2 copy-start.5
  60.4 3.4 %copy-start.6 = (bf16[256,256]{1,0:T(8,128)(2,1)S(1)}, bf16[256,256]{1,0:T(8,128)(2,1)}, u32[]{:S(2)}) copy-start(bf16[256,256]{1,0:T(8,128)(2,1)} %param.15) | copy-start | bytes 393220
  65.3 4.5 %copy-start.7 = (bf16[256,256]{1,0:T(8,128)(2,1)S(1)}, bf16[256,256]{1,0:T(8,128)(2,1)}, u32[]{:S(2)}) copy-start(bf16[256,256]{1,0:T(8,128)(2,1)} %param.16) | copy-start | bytes 393220
  79.8 1.9 %copy-start.2 = (bf16[64,32,4,64]{3,2,1,0:T(4,128)(2,1)S(1)}, bf16[64,32,4,64]{3,2,1,0:T(4,128)(2,1)}, u32[]{:S(2)}) copy-start(bf16[64,32,4,64]{3,2,1,0:T(4,128)(2,1)} %reshape.59) | copy-start | bytes 3145732
  92.2 77.5 %all-to-all-start.1 = ((bf16[64,32,256]{2,1,0:T(8,128)(2,1)}), bf16[64,32,256]{2,1,0:T(8,128)(2,1)S(1)}, u32[]{:S(2)}, u32[]{:S(2)}) async-start(bf16[64,32,256]{2,1,0:T(8,128)(2,1)} %get-tuple-element.9), calls=%async_computation.1 | async-start | bytes 2097152 | tf_op jit(solution)/shard_map/all_to_all | solution.py:96
